TPU v7x, 32 devices: a whole 2x2x4 slice. The times are simulated.
32 devices in a mesh: section: 8 (over z, core), rows: 4 (over y, x).
Axes of the slice: x: 2, y: 2, z: 4, core: 2. Of those that a mesh axis runs over, the one named last changes fastest.
Arguments:
- activations: bfloat16 [8, 16, 32, 768], P('section', 'rows'), may hold values from -6 to 6
- cotangent: bfloat16 [8, 16, 32, 3072], P('section', None, None, 'rows'), may hold values from -6 to 6
- proj_weight: bfloat16 [768, 3072], P('section', 'rows'), may hold values from -0.21875 to 0.21875
- kernel_taps: bfloat16 [49, 768], replicated, may hold values from -0.875 to 0.875
- ln_gain: float32 [768], replicated, may hold values from 0.1 to 1.9
- ln_shift: float32 [768], replicated, may hold values from -3 to 3
- heights: int32 [8], P('section'), may hold values from 8 to 16, as said below
- widths: int32 [8], P('section'), may hold values from 16 to 32, as said below
Outputs:
- input_grad: bfloat16 [8, 16, 32, 768], P('section', 'rows')
- weight_grad: float32 [768, 3072], P('section', 'rows')
Inputs may be any that keep to these rules, and one draw needn't show every extreme that they name: `heights`: every image has at least half of 16 valid rows, and some image has all 16. `widths`: every image has at least half of 32 valid columns, and some image has all 32.
All inputs are finite; a program needn't handle non-finite values.
Results may differ from a plain program's by a relative error of at most 0.0049.
Values may be sent and summed in bfloat16 or wider, within the bound.
No kernel may reach another device: no remote copies, remote signals or barrier semaphores. Data moves between devices by JAX's collectives and lax.ppermute only.
A program may use at most 64 MiB of HBM per device.

v0:
```python
import functools

import jax
import jax.numpy as jnp
import numpy as np
from jax import lax
from jax.experimental import pallas as pl
from jax.experimental.pallas import tpu as pltpu
from jax.sharding import PartitionSpec as P

epsilon = 1e-06
LANES = 128
VECTOR = 240
SUBLANES = 8


TILE = 4


def cost(operations, moved):
    return pl.CostEstimate(flops=operations, bytes_accessed=moved, transcendentals=0)


def run(kernel, outs, args, scratch=(), estimate=None, aliases=None, name=None):
    held = list(args) + list(outs) + list(scratch)
    taken = sum(int(np.prod(value.shape)) * jnp.dtype(value.dtype).itemsize for value in held)
    vmem = pl.BlockSpec(memory_space=pltpu.VMEM)
    smem = pl.BlockSpec(memory_space=pltpu.SMEM)
    return pl.pallas_call(
        kernel,
        out_shape=tuple(outs),
        in_specs=[smem if arg.dtype == jnp.int32 else vmem for arg in args],
        out_specs=tuple(vmem for _ in outs),
        scratch_shapes=[pltpu.VMEM(value.shape, value.dtype) for value in scratch],
        input_output_aliases=aliases or {},
        compiler_params=pltpu.CompilerParams(vmem_limit_bytes=taken + taken // 8 + (4 << 20)),
        cost_estimate=estimate or cost(1, 1),
        name=name,
    )(*args)


def f32(*shape):
    return jax.ShapeDtypeStruct(shape, jnp.float32)


def bf16(*shape):
    return jax.ShapeDtypeStruct(shape, jnp.bfloat16)


def begin_kernel(out_ref):
    out_ref[...] = jnp.zeros(out_ref.shape, out_ref.dtype)


def prepare_kernel(zero_ref, high_ref, wid_ref, taps_ref, wide_ref, valid_ref):
    count, chans = taps_ref.shape
    taps = taps_ref[...].astype(jnp.float32)
    for tap in range(count):
        wide_ref[tap] = jnp.broadcast_to(taps[tap : tap + 1], (SUBLANES, chans))
    _, width, lanes = valid_ref.shape
    columns = lax.broadcasted_iota(jnp.int32, (width, lanes), 0) < wid_ref[0]

    @pl.loop(0, valid_ref.shape[0])
    def _(row):
        valid_ref[row] = jnp.where(columns & (row < high_ref[0]), 1.0, 0.0) + zero_ref[0:1, :]


def prepare(heights, widths, taps, height, width):
    count, chans = taps.shape
    outs = [f32(count, SUBLANES, chans), f32(height, width, LANES)]
    estimate = cost(VECTOR * 128 * taps.size, 1)
    zero = run(begin_kernel, [f32(SUBLANES, LANES)], (), estimate=estimate, name="begin")[0]
    args = (zero, heights, widths, taps)
    return run(prepare_kernel, outs, args, name="prepare")


def clear_sides(source, width):
    sides = jnp.zeros((source.shape[0], 8, LANES), source.dtype)
    source[:, :8, :] = sides
    source[:, 8 + width :, :] = sides


def conv_rows(load, positions, outs, wide_ref, lanes, width, flip):
    stride = width // SUBLANES
    running = {out: [None] * stride for out in outs}
    for row, position in enumerate(positions):
        users = [out for out in outs if 0 <= position - out <= 6]
        if not users:
            continue
        shifted = [load(row, pl.ds(5 + k, SUBLANES, stride=stride)) for k in range(stride + 6)]
        for out in users:
            for along in range(7):
                tap = (position - out) * 7 + along
                weight = wide_ref[48 - tap if flip else tap, :, lanes]
                for i in range(stride):
                    term = weight * shifted[i + along]
                    before = running[out][i]
                    running[out][i] = term if before is None else before + term
    return running


def forward_kernel(bands, indices, fresh, valid_ref, taps_ref, *refs):
    act_refs, (mixed, source) = refs[: len(indices)], refs[-2:]
    rows_dev, width, _ = act_refs[0].shape
    blocks, height = mixed.shape[0], mixed.shape[1] - 6
    stride = width // SUBLANES
    band = lax.axis_index("rows")
    joined = source.shape[0] // rows_dev
    clear_sides(source, width)
    once = fresh and len(indices) == joined
    firsts = [sender(band, index, bands) * rows_dev for index in indices]

    @pl.loop(0, blocks)
    def _(block):
        lanes = pl.ds(pl.multiple_of(block * LANES, LANES), LANES)
        if fresh:
            mixed[block] = jnp.zeros(mixed.shape[1:], mixed.dtype)
        for start in range(0, len(indices), joined):
            base = firsts[start]
            for first in firsts[start : start + joined]:
                base = jnp.minimum(base, first)
            for first, act_ref in zip(firsts[start:], act_refs[start : start + joined]):
                for i in range(rows_dev):
                    row = first + i
                    value = act_ref[i, :, lanes].astype(jnp.float32) * valid_ref[row]
                    source[row - base, 8 : 8 + width, :] = value
            rows = joined * rows_dev
            for low in range(0, rows + 6, TILE):
                outs = range(low, min(low + TILE, rows + 6))
                positions = [i + 6 for i in range(rows)]
                running = conv_rows(
                    lambda row, columns_of: source[row, columns_of, :],
                    positions, outs, taps_ref, lanes, width, False,
                )
                for out, pieces in running.items():
                    for i, value in enumerate(pieces):
                        columns_of = pl.ds(i, SUBLANES, stride=stride)
                        if not once:
                            value = value + mixed[block, base + out, columns_of, :]
                        mixed[block, base + out, columns_of, :] = value


def forward(valid, wide, acts, indices, bands, before=None):
    rows_dev, width, chans = acts[0].shape
    joined = 2 if bands & (bands - 1) == 0 and len(indices) % 2 == 0 else 1
    extra = () if before is None else (before,)
    return run(
        functools.partial(forward_kernel, bands, indices, before is None),
        [f32(chans // LANES, rows_dev * bands + 6, width, LANES)],
        (valid, wide, *acts, *extra),
        [f32(joined * rows_dev, width + 16, LANES)],
        cost(3 * VECTOR * len(acts) * acts[0].size * 49 * 2, 6 * len(acts) * acts[0].size),
        {2 + len(acts): 0} if extra else {},
        "forward",
    )[0]


def normalise_kernel(valid_ref, mixed, gain_ref, shift_ref, normed_ref, centres, spreads):
    blocks, height, width, _ = mixed.shape
    height = height - 6
    chans = blocks * LANES

    @pl.loop(0, height // TILE)
    def _(step):
        rows = [step * TILE + i for i in range(TILE)]
        sums = [sum(mixed[block, row + 3] for block in range(blocks)) for row in rows]
        for row, value in zip(rows, sums):
            centre = jnp.sum(value, axis=-1, keepdims=True) / chans
            centres[row] = jnp.broadcast_to(centre, (width, LANES))

    @pl.loop(0, height // TILE)
    def _(step):
        rows = [step * TILE + i for i in range(TILE)]
        sums = []
        for row in rows:
            centre = centres[row]
            away = [mixed[block, row + 3] - centre for block in range(blocks)]
            sums.append(sum(value * value for value in away))
        for row, value in zip(rows, sums):
            spread = jnp.sum(value, axis=-1, keepdims=True) / chans
            spreads[row] = jnp.broadcast_to(lax.rsqrt(spread + epsilon), (width, LANES))

    @pl.loop(0, height)
    def _(row):
        rows = pl.ds(pl.multiple_of(row * width, width), width)
        centre, inv = centres[row], spreads[row]
        for block in range(blocks):
            lanes = slice(block * LANES, (block + 1) * LANES)
            unit = (mixed[block, row + 3] - centre) * inv
            value = unit * gain_ref[block : block + 1, :] + shift_ref[block : block + 1, :]
            value = value * valid_ref[row]
            normed_ref[rows, lanes] = value.astype(normed_ref.dtype)


def normalise(valid, mixed, gain, shift):
    blocks, height, width, _ = mixed.shape
    height = height - 6
    outs = [bf16(height * width, blocks * LANES)] + [f32(height, width, LANES)] * 2
    return run(normalise_kernel, outs, (valid, mixed, gain, shift), name="normalise")


def project_kernel(groups, order, valid_ref, grad_ref, mixed, centres, spreads, gain_ref, *refs):
    mine_refs, other_refs = refs[:groups], refs[groups : 2 * groups]
    out_ref, whole, result, means, alongs = refs[2 * groups :]
    band = mine_refs[0].shape[0]
    blocks, height, width, _ = mixed.shape
    height = height - 6
    chans = blocks * LANES
    parity, place = parity_and_place()
    for refs_of, core in ((mine_refs, parity), (other_refs, 1 - parity)):
        for at, index in enumerate(order):
            step = sender(place, index, len(order))
            start = pl.multiple_of((2 * step + core) * band, 16)
            whole[pl.ds(start, band), :] = refs_of[at][...]
    result[...] = lax.dot_general(
        grad_ref[...], whole[...], (((1,), (1,)), ((), ())), preferred_element_type=jnp.float32
    )

    def scaled_unit(row, block):
        rows = pl.ds(pl.multiple_of(row * width, width), width)
        lanes = slice(block * LANES, (block + 1) * LANES)
        scaled = result[rows, lanes] * gain_ref[block : block + 1, :]
        return scaled, (mixed[block, row + 3] - centres[row]) * spreads[row]

    @pl.loop(0, height // TILE)
    def _(step):
        sums = []
        for i in range(TILE):
            row = step * TILE + i
            pairs = [scaled_unit(row, block) for block in range(blocks)]
            sums.append((row, sum(p[0] for p in pairs), sum(p[0] * p[1] for p in pairs)))
        for row, scaled, product in sums:
            mean = jnp.sum(scaled, axis=-1, keepdims=True) / chans
            means[row] = jnp.broadcast_to(mean, (width, LANES))
            along = jnp.sum(product, axis=-1, keepdims=True) / chans
            alongs[row] = jnp.broadcast_to(along, (width, LANES))

    @pl.loop(0, blocks)
    def _(block):
        clear_sides(out_ref.at[block], width)
        empty = jnp.zeros((3,) + out_ref.shape[2:], out_ref.dtype)
        out_ref[block, :3] = empty
        out_ref[block, 3 + height :] = empty

    @pl.loop(0, height)
    def _(row):
        mean, along = means[row], alongs[row]
        inv = spreads[row] * valid_ref[row]
        for block in range(blocks):
            scaled, unit = scaled_unit(row, block)
            out_ref[block, row + 3, 8 : 8 + width, :] = inv * (scaled - mean - unit * along)


def project(valid, grad, mixed, centres, spreads, gain, mine, other, order):
    blocks, height, width, _ = mixed.shape
    chans = blocks * LANES
    return run(
        functools.partial(project_kernel, len(mine), order),
        [f32(blocks, height, width + 16, LANES)],
        (valid, grad, mixed, centres, spreads, gain, *mine, *other),
        [bf16(chans, grad.shape[1]), f32(grad.shape[0], chans)] + [f32(*centres.shape)] * 2,
        cost(VECTOR * mixed.size * 12, 8 * mixed.size),
        name="project",
    )[0]


def backward_kernel(index, bands, valid_ref, grad_ref, taps_ref, out_ref, result):
    rows_dev, width, chans = out_ref.shape
    stride = width // SUBLANES
    first = partner(lax.axis_index("rows"), index, bands) * rows_dev

    @pl.loop(0, chans // LANES)
    def _(block):
        lanes = pl.ds(pl.multiple_of(block * LANES, LANES), LANES)
        for low in range(0, rows_dev, TILE):
            outs = range(low, min(low + TILE, rows_dev))
            running = conv_rows(
                lambda row, columns_of: grad_ref[block, first + row, columns_of, :],
                list(range(rows_dev + 6)), outs, taps_ref, lanes, width, True,
            )
            for out, pieces in running.items():
                for i, value in enumerate(pieces):
                    result[out, pl.ds(i, SUBLANES, stride=stride), :] = value
        for row in range(rows_dev):
            out_ref[row, :, lanes] = (result[row] * valid_ref[first + row]).astype(out_ref.dtype)


def backward(valid, grad, taps, index, bands):
    blocks, height, width, _ = grad.shape
    rows_dev, width = (height - 6) // bands, width - 16
    shape = (rows_dev, width, blocks * LANES)
    return run(
        functools.partial(backward_kernel, index, bands),
        [bf16(*shape) if index else f32(*shape)],
        (valid, grad, taps),
        [f32(rows_dev, width, LANES)],
        cost(VECTOR * rows_dev * width * blocks * LANES * 49 * 2, 1),
        name="backward",
    )[0]


def outer_kernel(normed_ref, grad_ref, whole_ref, send_ref):
    pieces, band, hidden = whole_ref.shape
    parity, _ = parity_and_place()
    whole_ref[...] = lax.dot_general(
        normed_ref[...], grad_ref[...], (((0,), (0,)), ((), ())), preferred_element_type=jnp.float32
    ).reshape(pieces, band, hidden)
    for piece in range(pieces // 2):
        send_ref[piece] = whole_ref[2 * piece + 1 - parity].astype(send_ref.dtype)


def outer(normed, grad, count):
    chans, hidden = normed.shape[1], grad.shape[1]
    outs = [f32(count, chans // count, hidden), bf16(count // 2, chans // count, hidden)]
    return run(outer_kernel, outs, (normed, grad), name="outer")


def kept(held_ref, got_ref, level, parity, piece):
    held = held_ref[2 * piece + parity] if level == 1 else held_ref[piece]
    return held + got_ref[piece].astype(jnp.float32)


def fold_kernel(level, held_ref, got_ref, keep_ref, send_ref):
    parity, place = parity_and_place()
    bit = lax.rem(place >> level - 1, 2)
    for piece in range(keep_ref.shape[0]):
        keep_ref[piece] = kept(held_ref, got_ref, level, parity, 2 * piece + bit)
        sent = kept(held_ref, got_ref, level, parity, 2 * piece + 1 - bit)
        send_ref[piece] = sent.astype(send_ref.dtype)


def fold(held, got, level):
    pieces, band, hidden = got.shape
    outs = [f32(pieces // 2, band, hidden), bf16(pieces // 2, band, hidden)]
    return run(functools.partial(fold_kernel, level), outs, (held, got), name="fold")


def finish_kernel(count, parts, *refs):
    back_refs, weight_refs, (back_ref, weight_ref) = refs[:parts], refs[parts:-2], refs[-2:]

    def total(values):
        return sum(ref[...].astype(jnp.float32) for ref in values)

    back_ref[...] = total(back_refs).astype(back_ref.dtype)
    weight_ref[...] = total(weight_refs) / count


def finish(backs, weights, count):
    outs = [bf16(*backs[0].shape), f32(*weights[0].shape)]
    kernel = functools.partial(finish_kernel, count, len(backs))
    return run(kernel, outs, (*backs, *weights), name="finish")


def parity_and_place():
    index = lax.axis_index("section")
    return lax.rem(index, 2), index // 2


def partner(place, index, count):
    return place ^ index if count & (count - 1) == 0 else (place + index) % count


def sender(place, index, count):
    return place ^ index if count & (count - 1) == 0 else (place + count - index) % count


def swap_pairs(value):
    count = lax.axis_size("section")
    return lax.ppermute(value, "section", [(i, i ^ 1) for i in range(count)])


def send_rows(value, index):
    if index == 0:
        return value
    count = lax.axis_size("rows")
    return lax.ppermute(value, "rows", [(i, partner(i, index, count)) for i in range(count)])


def send_section(value, index):
    count = lax.axis_size("section")
    way = [(i, partner(i // 2, index, count // 2) * 2 + i % 2) for i in range(count)]
    return lax.ppermute(value, "section", way)


def gather_pairs(block, first):
    steps = lax.axis_size("section") // 2
    if steps & (steps - 1):
        return [block] + [send_section(block, i) for i in range(1, steps)], list(range(steps))
    pieces = {0: block}
    while len(pieces) < steps:
        far = steps // (2 * len(pieces))
        ready = {i: piece if i == 0 else after(piece, first) for i, piece in pieces.items()}
        pieces |= {i ^ far: send_section(piece, far) for i, piece in ready.items()}
    return list(pieces.values()), list(pieces)


def scatter_section(keep, send):
    count = lax.axis_size("section")
    level, sends = 0, [send]
    while True:
        way = [(i, i ^ 1 << level) for i in range(count)]
        got = lax.ppermute(send, "section", way)
        level += 1
        if got.shape[0] % 2:
            break
        keep, send = fold(keep, got, level)
        sends.append(send)
    rest = keep.shape[0]
    if rest == 1:
        return [keep[0], got[0]], sends
    total = keep + got.astype(jnp.float32)
    place = lax.axis_index("section") >> level
    result = lax.dynamic_index_in_dim(total, place, 0, keepdims=False)
    for shift in range(1, rest):
        piece = lax.dynamic_index_in_dim(total, (place + shift) % rest, 0, keepdims=False)
        way = [(i, (i + (shift << level)) % count) for i in range(count)]
        result = result + lax.ppermute(piece.astype(jnp.bfloat16), "section", way).astype(jnp.float32)
    return [result], sends


def after(value, *others):
    return lax.optimization_barrier((value, others))[0]


def local(activations, cotangent, proj_weight, kernel_taps, ln_gain, ln_shift, heights, widths):
    rows_dev, width_dev, chans = activations.shape[1:]
    height_all = cotangent.shape[1]
    hidden_dev = cotangent.shape[3]
    bands = lax.axis_size("rows")
    count = lax.axis_size("section")
    wide, valid = prepare(heights, widths, kernel_taps, height_all, width_dev)
    gain, shift = (value.reshape(chans // LANES, LANES) for value in (ln_gain, ln_shift))
    grad = cotangent.reshape(-1, hidden_dev)

    acts = [activations[0]] + [send_rows(activations[0], i) for i in range(1, bands)]
    half = bands // 2
    mixed = forward(valid, wide, acts[:half], range(half), bands)
    proj_mine, order = gather_pairs(proj_weight, mixed)
    mixed = forward(valid, wide, acts[half:], range(half, bands), bands, mixed)

    normed, centres, spreads = normalise(valid, mixed, gain, shift)
    whole, send = outer(normed, grad, count)
    weights, sends = scatter_section(whole, after(send, *proj_mine))

    proj_other = [swap_pairs(after(stack, normed)) for stack in proj_mine]
    grads = after(grad, sends[min(1, len(sends) - 1)])
    grad_mixed = project(valid, grads, mixed, centres, spreads, gain, proj_mine, proj_other, order)
    backs = []
    for i in [*range(2, bands), 1, 0]:
        ready = sends[min(1, len(sends) - 1)] if i > 1 else sends[-1]
        backs.append(send_rows(backward(after(valid, ready), grad_mixed, wide, i, bands), i))
    back, weight_grad = finish(backs, weights, count)
    return (back[None], weight_grad)


def solution(mesh):
    in_specs = (
        P("section", "rows", None, None),
        P("section", None, None, "rows"),
        P("section", "rows"),
        P(),
        P(),
        P(),
        P("section"),
        P("section"),
    )
    out_specs = (P("section", "rows", None, None), P("section", "rows"))
    return jax.shard_map(local, mesh=mesh, in_specs=in_specs, out_specs=out_specs, check_vma=False)
```

profile of v0, /device:TPU:0, one launch (start us, length us, event | category | flops | bytes accessed | tf_op | source)
XLA Modules:
  0.0 43.3 jit_solution(15306551199817250428)
XLA Ops:
  0.6 3.0 %collective-permute-start.2 = (bf16[4,32,768]{2,1,0:T(8,128)(2,1)}, bf16[4,32,768]{2,1,0:T(8,128)(2,1)S(1)}, u32[]{:S(2)}, u32[]{:S(2)}) collective-permute-start(bf16[4,32,768]{2,1,0:T(8,128)(2,1)} %bitcast.14), channel_id=1, source_target_pairs={{0,1},{1,0},{2,3},{3,2},{4,5},{5,4},{6,7},{7,6},{8,9},{9,8},{10,11... | collective-permute-start | bytes 589832 | tf_op jit(solution)/shard_map/ppermute | solution.py:375
  3.6 1.5 %collective-permute-start = (bf16[4,32,768]{2,1,0:T(8,128)(2,1)}, bf16[4,32,768]{2,1,0:T(8,128)(2,1)S(1)}, u32[]{:S(2)}, u32[]{:S(2)}) collective-permute-start(bf16[4,32,768]{2,1,0:T(8,128)(2,1)} %bitcast.15), channel_id=1, source_target_pairs={{0,2},{1,3},{2,0},{3,1},{4,6},{5,7},{6,4},{7,5},{8,10},{9,11},{10,... | collective-permute-start | bytes 589832 | tf_op jit(solution)/shard_map/ppermute | solution.py:375
  5.2 3.0 %collective-permute-start.3 = (bf16[96,768]{1,0:T(8,128)(2,1)}, bf16[96,768]{1,0:T(8,128)(2,1)S(1)}, u32[]{:S(2)}, u32[]{:S(2)}) collective-permute-start(bf16[96,768]{1,0:T(8,128)(2,1)} %refs_0_.1), channel_id=1, source_target_pairs={{0,16},{4,20},{8,24},{12,28},{16,0},{20,4},{24,8},{28,12},{1,17},{... | collective-permute-start | bytes 442376 | tf_op jit(solution)/shard_map/ppermute | solution.py:381
  8.2 1.6 %collective-permute-start.4 = (bf16[96,768]{1,0:T(8,128)(2,1)}, bf16[96,768]{1,0:T(8,128)(2,1)S(1)}, u32[]{:S(2)}, u32[]{:S(2)}) collective-permute-start(bf16[96,768]{1,0:T(8,128)(2,1)} %refs_0_.1), channel_id=1, source_target_pairs={{0,8},{4,12},{8,0},{12,4},{16,24},{20,28},{24,16},{28,20},{1,9},{5... | collective-permute-start | bytes 442376 | tf_op jit(solution)/shard_map/ppermute | solution.py:381
  11.4 0.6 %copy-done.5 = bf16[1,4,32,768]{3,2,1,0:T(8,128)(2,1)S(1)} copy-done((bf16[1,4,32,768]{3,2,1,0:T(8,128)(2,1)S(1)}, bf16[1,4,32,768]{3,2,1,0:T(8,128)(2,1)}, u32[]{:S(2)}) %copy-start.5) | copy-done | bytes 196632
  12.0 2.7 %forward.2.refs_2_ = f32[6,22,32,128]{3,2,1,0:T(8,128)S(1)} custom-call(f32[16,32,128]{2,1,0:T(8,128)S(1)} %get-tuple-element.42.valid_ref, f32[49,8,768]{2,1,0:T(8,128)S(1)} %get-tuple-element.25.taps_ref, bf16[4,32,768]{2,1,0:T(8,128)(2,1)S(1)} %bitcast.17, bf16[4,32,768]{2,1,0:T(8,128)(2,1)S(1)} %collective-permute-done.2.refs_1_), custom_call_target="tpu_custom_call" | custom-call | flops 13872660480 | bytes 1179648 | tf_op jit(solution)/shard_map/forward/pallas_call | solution.py:29
  14.8 0.6 %collective-permute-start.5 = (bf16[96,768]{1,0:T(8,128)(2,1)S(1)}, bf16[96,768]{1,0:T(8,128)(2,1)S(1)}, u32[]{:S(2)}, u32[]{:S(2)}) collective-permute-start(bf16[96,768]{1,0:T(8,128)(2,1)S(1)} %collective-permute-done.3.refs_1_), channel_id=1, source_target_pairs={{0,8},{4,12},{8,0},{12,4},{16,24},{20,28},{24,16},{28,20},{1,9},{5... | collective-permute-start | bytes 442376 | tf_op jit(solution)/shard_map/ppermute | solution.py:381
  15.4 2.7 %forward.3.mixed = f32[6,22,32,128]{3,2,1,0:T(8,128)S(1)} custom-call(f32[16,32,128]{2,1,0:T(8,128)S(1)} %get-tuple-element.42.valid_ref, f32[49,8,768]{2,1,0:T(8,128)S(1)} %get-tuple-element.25.taps_ref, bf16[4,32,768]{2,1,0:T(8,128)(2,1)S(1)} %collective-permute-done.refs_0_, ...), custom_call_target="tpu_custom_call", output_to_operand_aliasing={{}: (4, {})} | custom-call | flops 13872660480 | bytes 1179648 | tf_op jit(solution)/shard_map/forward/pallas_call | solution.py:29
  18.2 1.3 %normalise.1 = (bf16[512,768]{1,0:T(8,128)(2,1)S(1)}, f32[16,32,128]{2,1,0:T(8,128)S(1)}, f32[16,32,128]{2,1,0:T(8,128)S(1)}) custom-call(f32[16,32,128]{2,1,0:T(8,128)S(1)} %get-tuple-element.42.valid_ref, f32[6,22,32,128]{3,2,1,0:T(8,128)S(1)} %forward.3.mixed, f32[6,128]{1,0:T(8,128)S(1)} %bitcast.11, f32[6,128]{1,0:T(8,128)S(1)} %bitcast.13), custom_call_target="tpu_custom_call" | custom-call | flops 1 | bytes 1 | tf_op jit(solution)/shard_map/normalise/pallas_call | solution.py:29
  19.5 1.0 %outer.1 = (f32[8,96,768]{2,1,0:T(8,128)S(1)}, bf16[4,96,768]{2,1,0:T(8,128)(2,1)S(1)}) custom-call(bf16[512,768]{1,0:T(8,128)(2,1)S(1)} %get-tuple-element.26.normed_ref, bf16[512,768]{1,0:T(8,128)(2,1)S(1)} %bitcast.7), custom_call_target="tpu_custom_call" | custom-call | flops 1 | bytes 1 | tf_op jit(solution)/shard_map/outer/pallas_call | solution.py:29
  21.7 0.9 %collective-permute-done.6.got_ref = bf16[4,96,768]{2,1,0:T(8,128)(2,1)S(1)} collective-permute-done((bf16[4,96,768]{2,1,0:T(8,128)(2,1)S(1)}, bf16[4,96,768]{2,1,0:T(8,128)(2,1)S(1)}, u32[]{:S(2)}, u32[]{:S(2)}) %collective-permute-start.6) | collective-permute-done | bytes 589856 | tf_op jit(solution)/shard_map/ppermute | solution.py:401
  22.7 1.5 %collective-permute-start.13 = (bf16[2,96,768]{2,1,0:T(8,128)(2,1)S(1)}, bf16[2,96,768]{2,1,0:T(8,128)(2,1)S(1)}, u32[]{:S(2)}, u32[]{:S(2)}) collective-permute-start(bf16[2,96,768]{2,1,0:T(8,128)(2,1)S(1)} %get-tuple-element.31), channel_id=1, source_target_pairs={{0,8},{4,12},{8,0},{12,4},{16,24},{20,28},{24,16},{28,20},{1,9},{5... | collective-permute-start | bytes 884744 | tf_op jit(solution)/shard_map/ppermute | solution.py:401
  24.3 2.2 %project.1.grad_ref = f32[6,22,48,128]{3,2,1,0:T(8,128)S(1)} custom-call(f32[16,32,128]{2,1,0:T(8,128)S(1)} %get-tuple-element.42.valid_ref, bf16[512,768]{1,0:T(8,128)(2,1)S(1)} %bitcast.8, f32[6,22,32,128]{3,2,1,0:T(8,128)S(1)} %forward.3.mixed, f32[16,32,128]{2,1,0:T(8,128)S(1)} %get-tuple-element.34.centres, ...), custom_call_target="tpu_custom_call" | custom-call | flops 1557135360 | bytes 4325376 | tf_op jit(solution)/shard_map/project/pallas_call | solution.py:29
  26.5 1.3 %backward.5 = bf16[4,32,768]{2,1,0:T(8,128)(2,1)S(1)} custom-call(f32[16,32,128]{2,1,0:T(8,128)S(1)} %get-tuple-element.42.valid_ref, f32[6,22,48,128]{3,2,1,0:T(8,128)S(1)} %project.1.grad_ref, f32[49,8,768]{2,1,0:T(8,128)S(1)} %get-tuple-element.25.taps_ref), custom_call_target="tpu_custom_call" | custom-call | flops 2312110080 | bytes 1 | tf_op jit(solution)/shard_map/backward/pallas_call | solution.py:29
  27.8 2.5 %collective-permute-start.12 = (bf16[4,32,768]{2,1,0:T(8,128)(2,1)S(1)}, bf16[4,32,768]{2,1,0:T(8,128)(2,1)S(1)}, u32[]{:S(2)}, u32[]{:S(2)}) collective-permute-start(bf16[4,32,768]{2,1,0:T(8,128)(2,1)S(1)} %backward.5), channel_id=1, source_target_pairs={{0,3},{1,2},{2,1},{3,0},{4,7},{5,6},{6,5},{7,4},{8,11},{9,10},{10,... | collective-permute-start | bytes 589832 | tf_op jit(solution)/shard_map/ppermute | solution.py:375
  30.4 1.3 %backward.4 = bf16[4,32,768]{2,1,0:T(8,128)(2,1)S(1)} custom-call(f32[16,32,128]{2,1,0:T(8,128)S(1)} %get-tuple-element.42.valid_ref, f32[6,22,48,128]{3,2,1,0:T(8,128)S(1)} %project.1.grad_ref, f32[49,8,768]{2,1,0:T(8,128)S(1)} %get-tuple-element.25.taps_ref), custom_call_target="tpu_custom_call" | custom-call | flops 2312110080 | bytes 1 | tf_op jit(solution)/shard_map/backward/pallas_call | solution.py:29
  31.7 0.6 %collective-permute-start.11 = (bf16[4,32,768]{2,1,0:T(8,128)(2,1)S(1)}, bf16[4,32,768]{2,1,0:T(8,128)(2,1)S(1)}, u32[]{:S(2)}, u32[]{:S(2)}) collective-permute-start(bf16[4,32,768]{2,1,0:T(8,128)(2,1)S(1)} %backward.4), channel_id=1, source_target_pairs={{0,2},{1,3},{2,0},{3,1},{4,6},{5,7},{6,4},{7,5},{8,10},{9,11},{10,... | collective-permute-start | bytes 589832 | tf_op jit(solution)/shard_map/ppermute | solution.py:375
  32.3 3.0 %collective-permute-start.15 = (bf16[1,96,768]{2,1,0:T(8,128)(2,1)S(1)}, bf16[1,96,768]{2,1,0:T(8,128)(2,1)S(1)}, u32[]{:S(2)}, u32[]{:S(2)}) collective-permute-start(bf16[1,96,768]{2,1,0:T(8,128)(2,1)S(1)} %get-tuple-element.41), channel_id=1, source_target_pairs={{0,16},{4,20},{8,24},{12,28},{16,0},{20,4},{24,8},{28,12},{1,17},{... | collective-permute-start | bytes 442376 | tf_op jit(solution)/shard_map/ppermute | solution.py:401
  35.3 1.3 %backward.6 = bf16[4,32,768]{2,1,0:T(8,128)(2,1)S(1)} custom-call(f32[16,32,128]{2,1,0:T(8,128)S(1)} %get-tuple-element.42.valid_ref, f32[6,22,48,128]{3,2,1,0:T(8,128)S(1)} %project.1.grad_ref, f32[49,8,768]{2,1,0:T(8,128)S(1)} %get-tuple-element.25.taps_ref), custom_call_target="tpu_custom_call" | custom-call | flops 2312110080 | bytes 1 | tf_op jit(solution)/shard_map/backward/pallas_call | solution.py:29
  36.6 1.6 %collective-permute-start.14 = (bf16[4,32,768]{2,1,0:T(8,128)(2,1)S(1)}, bf16[4,32,768]{2,1,0:T(8,128)(2,1)S(1)}, u32[]{:S(2)}, u32[]{:S(2)}) collective-permute-start(bf16[4,32,768]{2,1,0:T(8,128)(2,1)S(1)} %backward.6), channel_id=1, source_target_pairs={{0,1},{1,0},{2,3},{3,2},{4,5},{5,4},{6,7},{7,6},{8,9},{9,8},{10,11... | collective-permute-start | bytes 589832 | tf_op jit(solution)/shard_map/ppermute | solution.py:375
  38.1 1.3 %backward.7.refs_3_ = f32[4,32,768]{2,1,0:T(8,128)S(1)} custom-call(f32[16,32,128]{2,1,0:T(8,128)S(1)} %get-tuple-element.42.valid_ref, f32[6,22,48,128]{3,2,1,0:T(8,128)S(1)} %project.1.grad_ref, f32[49,8,768]{2,1,0:T(8,128)S(1)} %get-tuple-element.25.taps_ref), custom_call_target="tpu_custom_call" | custom-call | flops 2312110080 | bytes 1 | tf_op jit(solution)/shard_map/backward/pallas_call | solution.py:29
  39.7 2.1 %collective-permute-done.15 = bf16[1,96,768]{2,1,0:T(8,128)(2,1)S(1)} collective-permute-done((bf16[1,96,768]{2,1,0:T(8,128)(2,1)S(1)}, bf16[1,96,768]{2,1,0:T(8,128)(2,1)S(1)}, u32[]{:S(2)}, u32[]{:S(2)}) %collective-permute-start.15) | collective-permute-done | bytes 147488 | tf_op jit(solution)/shard_map/ppermute | solution.py:401
  41.7 0.7 %collective-permute-done.14.refs_2_ = bf16[4,32,768]{2,1,0:T(8,128)(2,1)S(1)} collective-permute-done((bf16[4,32,768]{2,1,0:T(8,128)(2,1)S(1)}, bf16[4,32,768]{2,1,0:T(8,128)(2,1)S(1)}, u32[]{:S(2)}, u32[]{:S(2)}) %collective-permute-start.14) | collective-permute-done | bytes 196640 | tf_op jit(solution)/shard_map/ppermute | solution.py:375
  42.5 0.9 %finish.1 = (bf16[4,32,768]{2,1,0:T(8,128)(2,1)}, f32[96,768]{1,0:T(8,128)}) custom-call(bf16[4,32,768]{2,1,0:T(8,128)(2,1)S(1)} %collective-permute-done.11.refs_0_, bf16[4,32,768]{2,1,0:T(8,128)(2,1)S(1)} %collective-permute-done.12.refs_1_, bf16[4,32,768]{2,1,0:T(8,128)(2,1)S(1)} %collective-permute-done.14.refs_2_, f32[4,32,768]{2,1,0:T(8,128)S(1)} %backward.7.refs_3_, ...), custom_call_target="tpu_custom_call" | custom-call | flops 1 | bytes 1 | tf_op jit(solution)/shard_map/finish/pallas_call | solution.py:29
  (34 shorter events, 1.9 us)
Async XLA Ops:
  0.6 10.5 %copy-start.2 = (bf16[49,768]{1,0:T(8,128)(2,1)S(1)}, bf16[49,768]{1,0:T(8,128)(2,1)}, u32[]{:S(2)}) copy-start(bf16[49,768]{1,0:T(8,128)(2,1)} %taps_ref.1) | copy-start | bytes 225796
  0.6 10.7 %collective-permute-start.2 = (bf16[4,32,768]{2,1,0:T(8,128)(2,1)}, bf16[4,32,768]{2,1,0:T(8,128)(2,1)S(1)}, u32[]{:S(2)}, u32[]{:S(2)}) collective-permute-start(bf16[4,32,768]{2,1,0:T(8,128)(2,1)} %bitcast.14), channel_id=1, source_target_pairs={{0,1},{1,0},{2,3},{3,2},{4,5},{5,4},{6,7},{7,6},{8,9},{9,8},{10,11... | collective-permute-start | bytes 589832 | tf_op jit(solution)/shard_map/ppermute | solution.py:375
  3.6 11.8 %collective-permute-start = (bf16[4,32,768]{2,1,0:T(8,128)(2,1)}, bf16[4,32,768]{2,1,0:T(8,128)(2,1)S(1)}, u32[]{:S(2)}, u32[]{:S(2)}) collective-permute-start(bf16[4,32,768]{2,1,0:T(8,128)(2,1)} %bitcast.15), channel_id=1, source_target_pairs={{0,2},{1,3},{2,0},{3,1},{4,6},{5,7},{6,4},{7,5},{8,10},{9,11},{10,... | collective-permute-start | bytes 589832 | tf_op jit(solution)/shard_map/ppermute | solution.py:375
  5.2 10.3 %collective-permute-start.1 = (bf16[4,32,768]{2,1,0:T(8,128)(2,1)}, bf16[4,32,768]{2,1,0:T(8,128)(2,1)S(1)}, u32[]{:S(2)}, u32[]{:S(2)}) collective-permute-start(bf16[4,32,768]{2,1,0:T(8,128)(2,1)} %bitcast.16), channel_id=1, source_target_pairs={{0,3},{1,2},{2,1},{3,0},{4,7},{5,6},{6,5},{7,4},{8,11},{9,10},{10,... | collective-permute-start | bytes 589832 | tf_op jit(solution)/shard_map/ppermute | solution.py:375
  5.2 9.6 %collective-permute-start.3 = (bf16[96,768]{1,0:T(8,128)(2,1)}, bf16[96,768]{1,0:T(8,128)(2,1)S(1)}, u32[]{:S(2)}, u32[]{:S(2)}) collective-permute-start(bf16[96,768]{1,0:T(8,128)(2,1)} %refs_0_.1), channel_id=1, source_target_pairs={{0,16},{4,20},{8,24},{12,28},{16,0},{20,4},{24,8},{28,12},{1,17},{... | collective-permute-start | bytes 442376 | tf_op jit(solution)/shard_map/ppermute | solution.py:381
  8.2 12.3 %collective-permute-start.4 = (bf16[96,768]{1,0:T(8,128)(2,1)}, bf16[96,768]{1,0:T(8,128)(2,1)S(1)}, u32[]{:S(2)}, u32[]{:S(2)}) collective-permute-start(bf16[96,768]{1,0:T(8,128)(2,1)} %refs_0_.1), channel_id=1, source_target_pairs={{0,8},{4,12},{8,0},{12,4},{16,24},{20,28},{24,16},{28,20},{1,9},{5... | collective-permute-start | bytes 442376 | tf_op jit(solution)/shard_map/ppermute | solution.py:381
  11.1 0.9 %copy-start.5 = (bf16[1,4,32,768]{3,2,1,0:T(8,128)(2,1)S(1)}, bf16[1,4,32,768]{3,2,1,0:T(8,128)(2,1)}, u32[]{:S(2)}) copy-start(bf16[1,4,32,768]{3,2,1,0:T(8,128)(2,1)} %param.8) | copy-start | bytes 589828
  14.8 3.4 %copy-start.3 = (f32[768]{0:T(1024)S(1)}, f32[768]{0:T(1024)}, u32[]{:S(2)}) copy-start(f32[768]{0:T(1024)} %param.12) | copy-start | bytes 9220
  14.8 3.4 %copy-start.4 = (f32[768]{0:T(1024)S(1)}, f32[768]{0:T(1024)}, u32[]{:S(2)}) copy-start(f32[768]{0:T(1024)} %param.13) | copy-start | bytes 9220
  14.8 5.7 %collective-permute-start.5 = (bf16[96,768]{1,0:T(8,128)(2,1)S(1)}, bf16[96,768]{1,0:T(8,128)(2,1)S(1)}, u32[]{:S(2)}, u32[]{:S(2)}) collective-permute-start(bf16[96,768]{1,0:T(8,128)(2,1)S(1)} %collective-permute-done.3.refs_1_), channel_id=1, source_target_pairs={{0,8},{4,12},{8,0},{12,4},{16,24},{20,28},{24,16},{28,20},{1,9},{5... | collective-permute-start | bytes 442376 | tf_op jit(solution)/shard_map/ppermute | solution.py:381
  18.2 1.3 %copy-start = (bf16[1,16,32,768]{3,2,1,0:T(8,128)(2,1)S(1)}, bf16[1,16,32,768]{3,2,1,0:T(8,128)(2,1)}, u32[]{:S(2)}) copy-start(bf16[1,16,32,768]{3,2,1,0:T(8,128)(2,1)} %param.9) | copy-start | bytes 2359300
  18.2 3.0 %copy-start.1 = (bf16[96,768]{1,0:T(8,128)(2,1)S(1)}, bf16[96,768]{1,0:T(8,128)(2,1)}, u32[]{:S(2)}) copy-start(bf16[96,768]{1,0:T(8,128)(2,1)} %refs_0_.1) | copy-start | bytes 442372
  20.5 2.1 %collective-permute-start.6 = (bf16[4,96,768]{2,1,0:T(8,128)(2,1)S(1)}, bf16[4,96,768]{2,1,0:T(8,128)(2,1)S(1)}, u32[]{:S(2)}, u32[]{:S(2)}) collective-permute-start(bf16[4,96,768]{2,1,0:T(8,128)(2,1)S(1)} %get-tuple-element.30), channel_id=1, source_target_pairs={{0,4},{4,0},{8,12},{12,8},{16,20},{20,16},{24,28},{28,24},{1,5},{5... | collective-permute-start | bytes 1769480 | tf_op jit(solution)/shard_map/ppermute | solution.py:401
  20.6 3.6 %collective-permute-start.8 = (bf16[96,768]{1,0:T(8,128)(2,1)S(1)}, bf16[96,768]{1,0:T(8,128)(2,1)S(1)}, u32[]{:S(2)}, u32[]{:S(2)}) collective-permute-start(bf16[96,768]{1,0:T(8,128)(2,1)S(1)} %collective-permute-done.3.refs_1_), channel_id=1, source_target_pairs={{0,4},{4,0},{8,12},{12,8},{16,20},{20,16},{24,28},{28,24},{1,5},{5... | collective-permute-start | bytes 442376 | tf_op jit(solution)/shard_map/ppermute | solution.py:368
  21.1 3.1 %collective-permute-start.9 = (bf16[96,768]{1,0:T(8,128)(2,1)S(1)}, bf16[96,768]{1,0:T(8,128)(2,1)S(1)}, u32[]{:S(2)}, u32[]{:S(2)}) collective-permute-start(bf16[96,768]{1,0:T(8,128)(2,1)S(1)} %collective-permute-done.4.refs_2_), channel_id=1, source_target_pairs={{0,4},{4,0},{8,12},{12,8},{16,20},{20,16},{24,28},{28,24},{1,5},{5... | collective-permute-start | bytes 442376 | tf_op jit(solution)/shard_map/ppermute | solution.py:368
  21.2 3.1 %collective-permute-start.7 = (bf16[96,768]{1,0:T(8,128)(2,1)S(1)}, bf16[96,768]{1,0:T(8,128)(2,1)S(1)}, u32[]{:S(2)}, u32[]{:S(2)}) collective-permute-start(bf16[96,768]{1,0:T(8,128)(2,1)S(1)} %copy-done.1), channel_id=1, source_target_pairs={{0,4},{4,0},{8,12},{12,8},{16,20},{20,16},{24,28},{28,24},{1,5},{5... | collective-permute-start | bytes 442376 | tf_op jit(solution)/shard_map/ppermute | solution.py:368
  21.6 2.6 %collective-permute-start.10 = (bf16[96,768]{1,0:T(8,128)(2,1)S(1)}, bf16[96,768]{1,0:T(8,128)(2,1)S(1)}, u32[]{:S(2)}, u32[]{:S(2)}) collective-permute-start(bf16[96,768]{1,0:T(8,128)(2,1)S(1)} %collective-permute-done.5.refs_3_), channel_id=1, source_target_pairs={{0,4},{4,0},{8,12},{12,8},{16,20},{20,16},{24,28},{28,24},{1,5},{5... | collective-permute-start | bytes 442376 | tf_op jit(solution)/shard_map/ppermute | solution.py:368
  22.7 9.5 %collective-permute-start.13 = (bf16[2,96,768]{2,1,0:T(8,128)(2,1)S(1)}, bf16[2,96,768]{2,1,0:T(8,128)(2,1)S(1)}, u32[]{:S(2)}, u32[]{:S(2)}) collective-permute-start(bf16[2,96,768]{2,1,0:T(8,128)(2,1)S(1)} %get-tuple-element.31), channel_id=1, source_target_pairs={{0,8},{4,12},{8,0},{12,4},{16,24},{20,28},{24,16},{28,20},{1,9},{5... | collective-permute-start | bytes 884744 | tf_op jit(solution)/shard_map/ppermute | solution.py:401
  27.8 11.6 %collective-permute-start.12 = (bf16[4,32,768]{2,1,0:T(8,128)(2,1)S(1)}, bf16[4,32,768]{2,1,0:T(8,128)(2,1)S(1)}, u32[]{:S(2)}, u32[]{:S(2)}) collective-permute-start(bf16[4,32,768]{2,1,0:T(8,128)(2,1)S(1)} %backward.5), channel_id=1, source_target_pairs={{0,3},{1,2},{2,1},{3,0},{4,7},{5,6},{6,5},{7,4},{8,11},{9,10},{10,... | collective-permute-start | bytes 589832 | tf_op jit(solution)/shard_map/ppermute | solution.py:375
  31.7 8.0 %collective-permute-start.11 = (bf16[4,32,768]{2,1,0:T(8,128)(2,1)S(1)}, bf16[4,32,768]{2,1,0:T(8,128)(2,1)S(1)}, u32[]{:S(2)}, u32[]{:S(2)}) collective-permute-start(bf16[4,32,768]{2,1,0:T(8,128)(2,1)S(1)} %backward.4), channel_id=1, source_target_pairs={{0,2},{1,3},{2,0},{3,1},{4,6},{5,7},{6,4},{7,5},{8,10},{9,11},{10,... | collective-permute-start | bytes 589832 | tf_op jit(solution)/shard_map/ppermute | solution.py:375
  32.3 9.4 %collective-permute-start.15 = (bf16[1,96,768]{2,1,0:T(8,128)(2,1)S(1)}, bf16[1,96,768]{2,1,0:T(8,128)(2,1)S(1)}, u32[]{:S(2)}, u32[]{:S(2)}) collective-permute-start(bf16[1,96,768]{2,1,0:T(8,128)(2,1)S(1)} %get-tuple-element.41), channel_id=1, source_target_pairs={{0,16},{4,20},{8,24},{12,28},{16,0},{20,4},{24,8},{28,12},{1,17},{... | collective-permute-start | bytes 442376 | tf_op jit(solution)/shard_map/ppermute | solution.py:401
  36.6 5.9 %collective-permute-start.14 = (bf16[4,32,768]{2,1,0:T(8,128)(2,1)S(1)}, bf16[4,32,768]{2,1,0:T(8,128)(2,1)S(1)}, u32[]{:S(2)}, u32[]{:S(2)}) collective-permute-start(bf16[4,32,768]{2,1,0:T(8,128)(2,1)S(1)} %backward.6), channel_id=1, source_target_pairs={{0,1},{1,0},{2,3},{3,2},{4,5},{5,4},{6,7},{7,6},{8,9},{9,8},{10,11... | collective-permute-start | bytes 589832 | tf_op jit(solution)/shard_map/ppermute | solution.py:375
where the time goes:
time: 43.5 us; the launch traced here: 43.3 us
  starting transfers between devices  20.1 us (46%)
  Pallas kernels  16.5 us (38%)
  waiting for transfers between devices  3.94 us (9%)
  between operations  2.14 us (5%)
  local copies, waits for them, and re-layouts  0.68 us (2%)
    pallas_call x14, Pallas kernels, run(): pl.pallas_call(kernel, out_shape=tuple(outs), in_specs=[smem if arg.dtype...  16.5 us
    ppermute x6, starting transfers between devices, send_rows(): lax.ppermute(value, 'rows', [(i, partner(i, index, count)) for i in range...  9.21 us
    ppermute x3, starting transfers between devices, send_section(): return lax.ppermute(value, 'section', way)  5.26 us
    ppermute x3, starting transfers between devices, scatter_section(): got = lax.ppermute(send, 'section', way)  4.54 us
    ppermute x3, waiting for transfers between devices, scatter_section(): got = lax.ppermute(send, 'section', way)  2.99 us
    ppermute x4, starting transfers between devices, swap_pairs(): return lax.ppermute(value, 'section', [(i, i ^ 1) for i in range(count)])  1.09 us
    ppermute x6, waiting for transfers between devices, send_rows(): lax.ppermute(value, 'rows', [(i, partner(i, index, count)) for i in range...  0.94 us
  transfers between devices with their start and end apart: 16, of which 4 were waited for; matrix products, arithmetic and copies ran while one was open for 0% of the time, Pallas kernels for 36%

commit v1 on v0

--- a/solution.py
+++ b/solution.py
@@ -51,7 +51,7 @@
     out_ref[...] = jnp.zeros(out_ref.shape, out_ref.dtype)
 
 
-def prepare_kernel(zero_ref, high_ref, wid_ref, taps_ref, wide_ref, valid_ref):
+def prepare_kernel(zero_ref, high_ref, wid_ref, taps_ref, act_ref, wide_ref, valid_ref):
     count, chans = taps_ref.shape
     taps = taps_ref[...].astype(jnp.float32)
     for tap in range(count):
@@ -64,12 +64,12 @@
         valid_ref[row] = jnp.where(columns & (row < high_ref[0]), 1.0, 0.0) + zero_ref[0:1, :]
 
 
-def prepare(heights, widths, taps, height, width):
+def prepare(heights, widths, taps, act, height):
     count, chans = taps.shape
-    outs = [f32(count, SUBLANES, chans), f32(height, width, LANES)]
+    outs = [f32(count, SUBLANES, chans), f32(height, act.shape[1], LANES)]
     estimate = cost(VECTOR * 128 * taps.size, 1)
     zero = run(begin_kernel, [f32(SUBLANES, LANES)], (), estimate=estimate, name="begin")[0]
-    args = (zero, heights, widths, taps)
+    args = (zero, heights, widths, taps, act)
     return run(prepare_kernel, outs, args, name="prepare")
 
 
@@ -148,7 +148,7 @@
         [f32(chans // LANES, rows_dev * bands + 6, width, LANES)],
         (valid, wide, *acts, *extra),
         [f32(joined * rows_dev, width + 16, LANES)],
-        cost(3 * VECTOR * len(acts) * acts[0].size * 49 * 2, 6 * len(acts) * acts[0].size),
+        cost(1, 1) if extra else cost(3 * VECTOR * len(acts) * acts[0].size * 49 * 2, 1),
         {2 + len(acts): 0} if extra else {},
         "forward",
     )[0]
@@ -198,19 +198,19 @@
     return run(normalise_kernel, outs, (valid, mixed, gain, shift), name="normalise")
 
 
-def project_kernel(groups, order, valid_ref, grad_ref, mixed, centres, spreads, gain_ref, *refs):
-    mine_refs, other_refs = refs[:groups], refs[groups : 2 * groups]
-    out_ref, whole, result, means, alongs = refs[2 * groups :]
+def project_kernel(steps, valid_ref, grad_ref, mixed, centres, spreads, gain_ref, *refs):
+    mine_refs, other_refs = refs[:steps], refs[steps : 2 * steps]
+    out_ref, whole, result, means, alongs = refs[2 * steps :]
     band = mine_refs[0].shape[0]
     blocks, height, width, _ = mixed.shape
     height = height - 6
     chans = blocks * LANES
     parity, place = parity_and_place()
     for refs_of, core in ((mine_refs, parity), (other_refs, 1 - parity)):
-        for at, index in enumerate(order):
-            step = sender(place, index, len(order))
+        for index, ref in enumerate(refs_of):
+            step = sender(place, index, steps)
             start = pl.multiple_of((2 * step + core) * band, 16)
-            whole[pl.ds(start, band), :] = refs_of[at][...]
+            whole[pl.ds(start, band), :] = ref[...]
     result[...] = lax.dot_general(
         grad_ref[...], whole[...], (((1,), (1,)), ((), ())), preferred_element_type=jnp.float32
     )
@@ -250,11 +250,11 @@
             out_ref[block, row + 3, 8 : 8 + width, :] = inv * (scaled - mean - unit * along)
 
 
-def project(valid, grad, mixed, centres, spreads, gain, mine, other, order):
+def project(valid, grad, mixed, centres, spreads, gain, mine, other):
     blocks, height, width, _ = mixed.shape
     chans = blocks * LANES
     return run(
-        functools.partial(project_kernel, len(mine), order),
+        functools.partial(project_kernel, len(mine)),
         [f32(blocks, height, width + 16, LANES)],
         (valid, grad, mixed, centres, spreads, gain, *mine, *other),
         [bf16(chans, grad.shape[1]), f32(grad.shape[0], chans)] + [f32(*centres.shape)] * 2,
@@ -381,16 +381,9 @@
     return lax.ppermute(value, "section", way)
 
 
-def gather_pairs(block, first):
+def gather_pairs(block):
     steps = lax.axis_size("section") // 2
-    if steps & (steps - 1):
-        return [block] + [send_section(block, i) for i in range(1, steps)], list(range(steps))
-    pieces = {0: block}
-    while len(pieces) < steps:
-        far = steps // (2 * len(pieces))
-        ready = {i: piece if i == 0 else after(piece, first) for i, piece in pieces.items()}
-        pieces |= {i ^ far: send_section(piece, far) for i, piece in ready.items()}
-    return list(pieces.values()), list(pieces)
+    return [block] + [send_section(block, index) for index in range(1, steps)]
 
 
 def scatter_section(keep, send):
@@ -427,15 +420,15 @@
     hidden_dev = cotangent.shape[3]
     bands = lax.axis_size("rows")
     count = lax.axis_size("section")
-    wide, valid = prepare(heights, widths, kernel_taps, height_all, width_dev)
+    wide, valid = prepare(heights, widths, kernel_taps, activations[0], height_all)
     gain, shift = (value.reshape(chans // LANES, LANES) for value in (ln_gain, ln_shift))
     grad = cotangent.reshape(-1, hidden_dev)
 
     acts = [activations[0]] + [send_rows(activations[0], i) for i in range(1, bands)]
     half = bands // 2
     mixed = forward(valid, wide, acts[:half], range(half), bands)
-    proj_mine, order = gather_pairs(proj_weight, mixed)
     mixed = forward(valid, wide, acts[half:], range(half, bands), bands, mixed)
+    proj_mine = gather_pairs(proj_weight)
 
     normed, centres, spreads = normalise(valid, mixed, gain, shift)
     whole, send = outer(normed, grad, count)
@@ -443,7 +436,7 @@
 
     proj_other = [swap_pairs(after(stack, normed)) for stack in proj_mine]
     grads = after(grad, sends[min(1, len(sends) - 1)])
-    grad_mixed = project(valid, grads, mixed, centres, spreads, gain, proj_mine, proj_other, order)
+    grad_mixed = project(valid, grads, mixed, centres, spreads, gain, proj_mine, proj_other)
     backs = []
     for i in [*range(2, bands), 1, 0]:
         ready = sends[min(1, len(sends) - 1)] if i > 1 else sends[-1]

time: 43.5 us -> 43.5 us (level)
    ppermute x3, starting transfers between devices: 5.26 us -> 6.36 us  [send_section(): return lax.ppermute(value, 'section', way)]
    ppermute x3, starting transfers between devices: 4.54 us -> 3.49 us  [scatter_section(): got = lax.ppermute(send, 'section', way)]
where the time goes in v1:
time: 43.5 us; the launch traced here: 43.4 us
  starting transfers between devices  20.1 us (46%)
  Pallas kernels  16.5 us (38%)
  waiting for transfers between devices  3.95 us (9%)
  between operations  2.16 us (5%)
  local copies, waits for them, and re-layouts  0.65 us (1%)
    pallas_call x14, Pallas kernels, run(): pl.pallas_call(kernel, out_shape=tuple(outs), in_specs=[smem if arg.dtype...  16.5 us
    ppermute x6, starting transfers between devices, send_rows(): lax.ppermute(value, 'rows', [(i, partner(i, index, count)) for i in range...  9.18 us
    ppermute x3, starting transfers between devices, send_section(): return lax.ppermute(value, 'section', way)  6.36 us
    ppermute x3, starting transfers between devices, scatter_section(): got = lax.ppermute(send, 'section', way)  3.49 us
    ppermute x3, waiting for transfers between devices, scatter_section(): got = lax.ppermute(send, 'section', way)  2.69 us
    ppermute x6, waiting for transfers between devices, send_rows(): lax.ppermute(value, 'rows', [(i, partner(i, index, count)) for i in range...  1.24 us
    ppermute x4, starting transfers between devices, swap_pairs(): return lax.ppermute(value, 'section', [(i, i ^ 1) for i in range(count)])  1.09 us
  transfers between devices with their start and end apart: 16, of which 4 were waited for; matrix products, arithmetic and copies ran while one was open for 0% of the time, Pallas kernels for 36%

profile of v1, /device:TPU:0, one launch (start us, length us, event | category | flops | bytes accessed | tf_op | source)
XLA Modules:
  0.0 43.4 jit_solution(9163079286866316917)
XLA Ops:
  0.7 3.0 %collective-permute-start.2 = (bf16[4,32,768]{2,1,0:T(8,128)(2,1)}, bf16[4,32,768]{2,1,0:T(8,128)(2,1)S(1)}, u32[]{:S(2)}, u32[]{:S(2)}) collective-permute-start(bf16[4,32,768]{2,1,0:T(8,128)(2,1)} %bitcast.10), channel_id=1, source_target_pairs={{0,1},{1,0},{2,3},{3,2},{4,5},{5,4},{6,7},{7,6},{8,9},{9,8},{10,11... | collective-permute-start | bytes 589832 | tf_op jit(solution)/shard_map/ppermute | solution.py:375
  3.7 1.5 %collective-permute-start = (bf16[4,32,768]{2,1,0:T(8,128)(2,1)}, bf16[4,32,768]{2,1,0:T(8,128)(2,1)S(1)}, u32[]{:S(2)}, u32[]{:S(2)}) collective-permute-start(bf16[4,32,768]{2,1,0:T(8,128)(2,1)} %bitcast.11), channel_id=1, source_target_pairs={{0,2},{1,3},{2,0},{3,1},{4,6},{5,7},{6,4},{7,5},{8,10},{9,11},{10,... | collective-permute-start | bytes 589832 | tf_op jit(solution)/shard_map/ppermute | solution.py:375
  5.2 2.0 %collective-permute-start.3 = (bf16[96,768]{1,0:T(8,128)(2,1)}, bf16[96,768]{1,0:T(8,128)(2,1)S(1)}, u32[]{:S(2)}, u32[]{:S(2)}) collective-permute-start(bf16[96,768]{1,0:T(8,128)(2,1)} %refs_0_.1), channel_id=1, source_target_pairs={{0,8},{4,12},{8,0},{12,4},{16,24},{20,28},{24,16},{28,20},{1,9},{5... | collective-permute-start | bytes 442376 | tf_op jit(solution)/shard_map/ppermute | solution.py:381
  7.2 2.6 %collective-permute-start.4 = (bf16[96,768]{1,0:T(8,128)(2,1)}, bf16[96,768]{1,0:T(8,128)(2,1)S(1)}, u32[]{:S(2)}, u32[]{:S(2)}) collective-permute-start(bf16[96,768]{1,0:T(8,128)(2,1)} %refs_0_.1), channel_id=1, source_target_pairs={{0,16},{4,20},{8,24},{12,28},{16,0},{20,4},{24,8},{28,12},{1,17},{... | collective-permute-start | bytes 442376 | tf_op jit(solution)/shard_map/ppermute | solution.py:381
  11.4 0.6 %copy-done.2 = bf16[96,768]{1,0:T(8,128)(2,1)S(1)} copy-done((bf16[96,768]{1,0:T(8,128)(2,1)S(1)}, bf16[96,768]{1,0:T(8,128)(2,1)}, u32[]{:S(2)}) %copy-start.2) | copy-done | bytes 147480
  12.0 1.7 %collective-permute-start.5 = (bf16[96,768]{1,0:T(8,128)(2,1)S(1)}, bf16[96,768]{1,0:T(8,128)(2,1)S(1)}, u32[]{:S(2)}, u32[]{:S(2)}) collective-permute-start(bf16[96,768]{1,0:T(8,128)(2,1)S(1)} %copy-done.2), channel_id=1, source_target_pairs={{0,24},{4,28},{8,16},{12,20},{16,8},{20,12},{24,0},{28,4},{1,25},{... | collective-permute-start | bytes 442376 | tf_op jit(solution)/shard_map/ppermute | solution.py:381
  13.8 2.7 %forward.2.refs_2_ = f32[6,22,32,128]{3,2,1,0:T(8,128)S(1)} custom-call(f32[16,32,128]{2,1,0:T(8,128)S(1)} %get-tuple-element.40.valid_ref, f32[49,8,768]{2,1,0:T(8,128)S(1)} %get-tuple-element.24.taps_ref, bf16[4,32,768]{2,1,0:T(8,128)(2,1)S(1)} %bitcast.14, bf16[4,32,768]{2,1,0:T(8,128)(2,1)S(1)} %collective-permute-done.2.refs_1_), custom_call_target="tpu_custom_call" | custom-call | flops 13872660480 | bytes 1 | tf_op jit(solution)/shard_map/forward/pallas_call | solution.py:29
  16.5 2.7 %forward.3.mixed = f32[6,22,32,128]{3,2,1,0:T(8,128)S(1)} custom-call(f32[16,32,128]{2,1,0:T(8,128)S(1)} %get-tuple-element.40.valid_ref, f32[49,8,768]{2,1,0:T(8,128)S(1)} %get-tuple-element.24.taps_ref, bf16[4,32,768]{2,1,0:T(8,128)(2,1)S(1)} %collective-permute-done.refs_0_, ...), custom_call_target="tpu_custom_call", output_to_operand_aliasing={{}: (4, {})} | custom-call | flops 1 | bytes 1 | tf_op jit(solution)/shard_map/forward/pallas_call | solution.py:29
  19.3 1.3 %normalise.1 = (bf16[512,768]{1,0:T(8,128)(2,1)S(1)}, f32[16,32,128]{2,1,0:T(8,128)S(1)}, f32[16,32,128]{2,1,0:T(8,128)S(1)}) custom-call(f32[16,32,128]{2,1,0:T(8,128)S(1)} %get-tuple-element.40.valid_ref, f32[6,22,32,128]{3,2,1,0:T(8,128)S(1)} %forward.3.mixed, f32[6,128]{1,0:T(8,128)S(1)} %bitcast.16, f32[6,128]{1,0:T(8,128)S(1)} %bitcast.18), custom_call_target="tpu_custom_call" | custom-call | flops 1 | bytes 1 | tf_op jit(solution)/shard_map/normalise/pallas_call | solution.py:29
  20.6 1.0 %outer.1 = (f32[8,96,768]{2,1,0:T(8,128)S(1)}, bf16[4,96,768]{2,1,0:T(8,128)(2,1)S(1)}) custom-call(bf16[512,768]{1,0:T(8,128)(2,1)S(1)} %get-tuple-element.25.normed_ref, bf16[512,768]{1,0:T(8,128)(2,1)S(1)} %bitcast.7), custom_call_target="tpu_custom_call" | custom-call | flops 1 | bytes 1 | tf_op jit(solution)/shard_map/outer/pallas_call | solution.py:29
  22.8 0.9 %collective-permute-done.6.got_ref = bf16[4,96,768]{2,1,0:T(8,128)(2,1)S(1)} collective-permute-done((bf16[4,96,768]{2,1,0:T(8,128)(2,1)S(1)}, bf16[4,96,768]{2,1,0:T(8,128)(2,1)S(1)}, u32[]{:S(2)}, u32[]{:S(2)}) %collective-permute-start.6) | collective-permute-done | bytes 589856 | tf_op jit(solution)/shard_map/ppermute | solution.py:394
  23.8 1.3 %collective-permute-start.13 = (bf16[2,96,768]{2,1,0:T(8,128)(2,1)S(1)}, bf16[2,96,768]{2,1,0:T(8,128)(2,1)S(1)}, u32[]{:S(2)}, u32[]{:S(2)}) collective-permute-start(bf16[2,96,768]{2,1,0:T(8,128)(2,1)S(1)} %get-tuple-element.29), channel_id=1, source_target_pairs={{0,8},{4,12},{8,0},{12,4},{16,24},{20,28},{24,16},{28,20},{1,9},{5... | collective-permute-start | bytes 884744 | tf_op jit(solution)/shard_map/ppermute | solution.py:394
  25.1 2.2 %project.1.grad_ref = f32[6,22,48,128]{3,2,1,0:T(8,128)S(1)} custom-call(f32[16,32,128]{2,1,0:T(8,128)S(1)} %get-tuple-element.40.valid_ref, bf16[512,768]{1,0:T(8,128)(2,1)S(1)} %bitcast.8, f32[6,22,32,128]{3,2,1,0:T(8,128)S(1)} %forward.3.mixed, f32[16,32,128]{2,1,0:T(8,128)S(1)} %get-tuple-element.32.centres, ...), custom_call_target="tpu_custom_call" | custom-call | flops 1557135360 | bytes 4325376 | tf_op jit(solution)/shard_map/project/pallas_call | solution.py:29
  27.4 1.3 %backward.5 = bf16[4,32,768]{2,1,0:T(8,128)(2,1)S(1)} custom-call(f32[16,32,128]{2,1,0:T(8,128)S(1)} %get-tuple-element.40.valid_ref, f32[6,22,48,128]{3,2,1,0:T(8,128)S(1)} %project.1.grad_ref, f32[49,8,768]{2,1,0:T(8,128)S(1)} %get-tuple-element.24.taps_ref), custom_call_target="tpu_custom_call" | custom-call | flops 2312110080 | bytes 1 | tf_op jit(solution)/shard_map/backward/pallas_call | solution.py:29
  28.7 2.5 %collective-permute-start.12 = (bf16[4,32,768]{2,1,0:T(8,128)(2,1)S(1)}, bf16[4,32,768]{2,1,0:T(8,128)(2,1)S(1)}, u32[]{:S(2)}, u32[]{:S(2)}) collective-permute-start(bf16[4,32,768]{2,1,0:T(8,128)(2,1)S(1)} %backward.5), channel_id=1, source_target_pairs={{0,3},{1,2},{2,1},{3,0},{4,7},{5,6},{6,5},{7,4},{8,11},{9,10},{10,... | collective-permute-start | bytes 589832 | tf_op jit(solution)/shard_map/ppermute | solution.py:375
  31.2 1.3 %backward.4 = bf16[4,32,768]{2,1,0:T(8,128)(2,1)S(1)} custom-call(f32[16,32,128]{2,1,0:T(8,128)S(1)} %get-tuple-element.40.valid_ref, f32[6,22,48,128]{3,2,1,0:T(8,128)S(1)} %project.1.grad_ref, f32[49,8,768]{2,1,0:T(8,128)S(1)} %get-tuple-element.24.taps_ref), custom_call_target="tpu_custom_call" | custom-call | flops 2312110080 | bytes 1 | tf_op jit(solution)/shard_map/backward/pallas_call | solution.py:29
  32.5 0.6 %collective-permute-start.11 = (bf16[4,32,768]{2,1,0:T(8,128)(2,1)S(1)}, bf16[4,32,768]{2,1,0:T(8,128)(2,1)S(1)}, u32[]{:S(2)}, u32[]{:S(2)}) collective-permute-start(bf16[4,32,768]{2,1,0:T(8,128)(2,1)S(1)} %backward.4), channel_id=1, source_target_pairs={{0,2},{1,3},{2,0},{3,1},{4,6},{5,7},{6,4},{7,5},{8,10},{9,11},{10,... | collective-permute-start | bytes 589832 | tf_op jit(solution)/shard_map/ppermute | solution.py:375
  33.1 2.1 %collective-permute-start.15 = (bf16[1,96,768]{2,1,0:T(8,128)(2,1)S(1)}, bf16[1,96,768]{2,1,0:T(8,128)(2,1)S(1)}, u32[]{:S(2)}, u32[]{:S(2)}) collective-permute-start(bf16[1,96,768]{2,1,0:T(8,128)(2,1)S(1)} %get-tuple-element.39), channel_id=1, source_target_pairs={{0,16},{4,20},{8,24},{12,28},{16,0},{20,4},{24,8},{28,12},{1,17},{... | collective-permute-start | bytes 442376 | tf_op jit(solution)/shard_map/ppermute | solution.py:394
  35.3 1.3 %backward.6 = bf16[4,32,768]{2,1,0:T(8,128)(2,1)S(1)} custom-call(f32[16,32,128]{2,1,0:T(8,128)S(1)} %get-tuple-element.40.valid_ref, f32[6,22,48,128]{3,2,1,0:T(8,128)S(1)} %project.1.grad_ref, f32[49,8,768]{2,1,0:T(8,128)S(1)} %get-tuple-element.24.taps_ref), custom_call_target="tpu_custom_call" | custom-call | flops 2312110080 | bytes 1 | tf_op jit(solution)/shard_map/backward/pallas_call | solution.py:29
  36.6 1.6 %collective-permute-start.14 = (bf16[4,32,768]{2,1,0:T(8,128)(2,1)S(1)}, bf16[4,32,768]{2,1,0:T(8,128)(2,1)S(1)}, u32[]{:S(2)}, u32[]{:S(2)}) collective-permute-start(bf16[4,32,768]{2,1,0:T(8,128)(2,1)S(1)} %backward.6), channel_id=1, source_target_pairs={{0,1},{1,0},{2,3},{3,2},{4,5},{5,4},{6,7},{7,6},{8,9},{9,8},{10,11... | collective-permute-start | bytes 589832 | tf_op jit(solution)/shard_map/ppermute | solution.py:375
  38.1 1.3 %backward.7.refs_3_ = f32[4,32,768]{2,1,0:T(8,128)S(1)} custom-call(f32[16,32,128]{2,1,0:T(8,128)S(1)} %get-tuple-element.40.valid_ref, f32[6,22,48,128]{3,2,1,0:T(8,128)S(1)} %project.1.grad_ref, f32[49,8,768]{2,1,0:T(8,128)S(1)} %get-tuple-element.24.taps_ref), custom_call_target="tpu_custom_call" | custom-call | flops 2312110080 | bytes 1 | tf_op jit(solution)/shard_map/backward/pallas_call | solution.py:29
  39.5 1.1 %collective-permute-done.11.refs_0_ = bf16[4,32,768]{2,1,0:T(8,128)(2,1)S(1)} collective-permute-done((bf16[4,32,768]{2,1,0:T(8,128)(2,1)S(1)}, bf16[4,32,768]{2,1,0:T(8,128)(2,1)S(1)}, u32[]{:S(2)}, u32[]{:S(2)}) %collective-permute-start.11) | collective-permute-done | bytes 196640 | tf_op jit(solution)/shard_map/ppermute | solution.py:375
  40.5 1.8 %collective-permute-done.15 = bf16[1,96,768]{2,1,0:T(8,128)(2,1)S(1)} collective-permute-done((bf16[1,96,768]{2,1,0:T(8,128)(2,1)S(1)}, bf16[1,96,768]{2,1,0:T(8,128)(2,1)S(1)}, u32[]{:S(2)}, u32[]{:S(2)}) %collective-permute-start.15) | collective-permute-done | bytes 147488 | tf_op jit(solution)/shard_map/ppermute | solution.py:394
  42.5 0.9 %finish.1 = (bf16[4,32,768]{2,1,0:T(8,128)(2,1)}, f32[96,768]{1,0:T(8,128)}) custom-call(bf16[4,32,768]{2,1,0:T(8,128)(2,1)S(1)} %collective-permute-done.11.refs_0_, bf16[4,32,768]{2,1,0:T(8,128)(2,1)S(1)} %collective-permute-done.12.refs_1_, bf16[4,32,768]{2,1,0:T(8,128)(2,1)S(1)} %collective-permute-done.14.refs_2_, f32[4,32,768]{2,1,0:T(8,128)S(1)} %backward.7.refs_3_, ...), custom_call_target="tpu_custom_call" | custom-call | flops 1 | bytes 1 | tf_op jit(solution)/shard_map/finish/pallas_call | solution.py:29
  (34 shorter events, 1.8 us)
Async XLA Ops:
  0.6 10.5 %copy-start.1 = (bf16[1,4,32,768]{3,2,1,0:T(8,128)(2,1)S(1)}, bf16[1,4,32,768]{3,2,1,0:T(8,128)(2,1)}, u32[]{:S(2)}) copy-start(bf16[1,4,32,768]{3,2,1,0:T(8,128)(2,1)} %param.8) | copy-start | bytes 589828
  0.6 10.5 %copy-start.3 = (bf16[49,768]{1,0:T(8,128)(2,1)S(1)}, bf16[49,768]{1,0:T(8,128)(2,1)}, u32[]{:S(2)}) copy-start(bf16[49,768]{1,0:T(8,128)(2,1)} %taps_ref.1) | copy-start | bytes 225796
  0.7 10.7 %collective-permute-start.2 = (bf16[4,32,768]{2,1,0:T(8,128)(2,1)}, bf16[4,32,768]{2,1,0:T(8,128)(2,1)S(1)}, u32[]{:S(2)}, u32[]{:S(2)}) collective-permute-start(bf16[4,32,768]{2,1,0:T(8,128)(2,1)} %bitcast.10), channel_id=1, source_target_pairs={{0,1},{1,0},{2,3},{3,2},{4,5},{5,4},{6,7},{7,6},{8,9},{9,8},{10,11... | collective-permute-start | bytes 589832 | tf_op jit(solution)/shard_map/ppermute | solution.py:375
  3.7 12.9 %collective-permute-start = (bf16[4,32,768]{2,1,0:T(8,128)(2,1)}, bf16[4,32,768]{2,1,0:T(8,128)(2,1)S(1)}, u32[]{:S(2)}, u32[]{:S(2)}) collective-permute-start(bf16[4,32,768]{2,1,0:T(8,128)(2,1)} %bitcast.11), channel_id=1, source_target_pairs={{0,2},{1,3},{2,0},{3,1},{4,6},{5,7},{6,4},{7,5},{8,10},{9,11},{10,... | collective-permute-start | bytes 589832 | tf_op jit(solution)/shard_map/ppermute | solution.py:375
  5.2 11.4 %collective-permute-start.1 = (bf16[4,32,768]{2,1,0:T(8,128)(2,1)}, bf16[4,32,768]{2,1,0:T(8,128)(2,1)S(1)}, u32[]{:S(2)}, u32[]{:S(2)}) collective-permute-start(bf16[4,32,768]{2,1,0:T(8,128)(2,1)} %bitcast.12), channel_id=1, source_target_pairs={{0,3},{1,2},{2,1},{3,0},{4,7},{5,6},{6,5},{7,4},{8,11},{9,10},{10,... | collective-permute-start | bytes 589832 | tf_op jit(solution)/shard_map/ppermute | solution.py:375
  5.2 16.4 %collective-permute-start.3 = (bf16[96,768]{1,0:T(8,128)(2,1)}, bf16[96,768]{1,0:T(8,128)(2,1)S(1)}, u32[]{:S(2)}, u32[]{:S(2)}) collective-permute-start(bf16[96,768]{1,0:T(8,128)(2,1)} %refs_0_.1), channel_id=1, source_target_pairs={{0,8},{4,12},{8,0},{12,4},{16,24},{20,28},{24,16},{28,20},{1,9},{5... | collective-permute-start | bytes 442376 | tf_op jit(solution)/shard_map/ppermute | solution.py:381
  7.2 14.4 %collective-permute-start.4 = (bf16[96,768]{1,0:T(8,128)(2,1)}, bf16[96,768]{1,0:T(8,128)(2,1)S(1)}, u32[]{:S(2)}, u32[]{:S(2)}) collective-permute-start(bf16[96,768]{1,0:T(8,128)(2,1)} %refs_0_.1), channel_id=1, source_target_pairs={{0,16},{4,20},{8,24},{12,28},{16,0},{20,4},{24,8},{28,12},{1,17},{... | collective-permute-start | bytes 442376 | tf_op jit(solution)/shard_map/ppermute | solution.py:381
  11.1 0.9 %copy-start.2 = (bf16[96,768]{1,0:T(8,128)(2,1)S(1)}, bf16[96,768]{1,0:T(8,128)(2,1)}, u32[]{:S(2)}) copy-start(bf16[96,768]{1,0:T(8,128)(2,1)} %refs_0_.1) | copy-start | bytes 442372
  12.0 9.6 %collective-permute-start.5 = (bf16[96,768]{1,0:T(8,128)(2,1)S(1)}, bf16[96,768]{1,0:T(8,128)(2,1)S(1)}, u32[]{:S(2)}, u32[]{:S(2)}) collective-permute-start(bf16[96,768]{1,0:T(8,128)(2,1)S(1)} %copy-done.2), channel_id=1, source_target_pairs={{0,24},{4,28},{8,16},{12,20},{16,8},{20,12},{24,0},{28,4},{1,25},{... | collective-permute-start | bytes 442376 | tf_op jit(solution)/shard_map/ppermute | solution.py:381
  16.5 2.8 %copy-start.4 = (f32[768]{0:T(1024)S(1)}, f32[768]{0:T(1024)}, u32[]{:S(2)}) copy-start(f32[768]{0:T(1024)} %param.12) | copy-start | bytes 9220
  16.5 2.8 %copy-start.5 = (f32[768]{0:T(1024)S(1)}, f32[768]{0:T(1024)}, u32[]{:S(2)}) copy-start(f32[768]{0:T(1024)} %param.13) | copy-start | bytes 9220
  19.3 1.3 %copy-start = (bf16[1,16,32,768]{3,2,1,0:T(8,128)(2,1)S(1)}, bf16[1,16,32,768]{3,2,1,0:T(8,128)(2,1)}, u32[]{:S(2)}) copy-start(bf16[1,16,32,768]{3,2,1,0:T(8,128)(2,1)} %param.9) | copy-start | bytes 2359300
  21.6 2.1 %collective-permute-start.6 = (bf16[4,96,768]{2,1,0:T(8,128)(2,1)S(1)}, bf16[4,96,768]{2,1,0:T(8,128)(2,1)S(1)}, u32[]{:S(2)}, u32[]{:S(2)}) collective-permute-start(bf16[4,96,768]{2,1,0:T(8,128)(2,1)S(1)} %get-tuple-element.28), channel_id=1, source_target_pairs={{0,4},{4,0},{8,12},{12,8},{16,20},{20,16},{24,28},{28,24},{1,5},{5... | collective-permute-start | bytes 1769480 | tf_op jit(solution)/shard_map/ppermute | solution.py:394
  21.7 3.4 %collective-permute-start.10 = (bf16[96,768]{1,0:T(8,128)(2,1)S(1)}, bf16[96,768]{1,0:T(8,128)(2,1)S(1)}, u32[]{:S(2)}, u32[]{:S(2)}) collective-permute-start(bf16[96,768]{1,0:T(8,128)(2,1)S(1)} %collective-permute-done.5.refs_3_), channel_id=1, source_target_pairs={{0,4},{4,0},{8,12},{12,8},{16,20},{20,16},{24,28},{28,24},{1,5},{5... | collective-permute-start | bytes 442376 | tf_op jit(solution)/shard_map/ppermute | solution.py:368
  22.2 2.9 %collective-permute-start.8 = (bf16[96,768]{1,0:T(8,128)(2,1)S(1)}, bf16[96,768]{1,0:T(8,128)(2,1)S(1)}, u32[]{:S(2)}, u32[]{:S(2)}) collective-permute-start(bf16[96,768]{1,0:T(8,128)(2,1)S(1)} %collective-permute-done.3.refs_1_), channel_id=1, source_target_pairs={{0,4},{4,0},{8,12},{12,8},{16,20},{20,16},{24,28},{28,24},{1,5},{5... | collective-permute-start | bytes 442376 | tf_op jit(solution)/shard_map/ppermute | solution.py:368
  22.3 2.8 %collective-permute-start.9 = (bf16[96,768]{1,0:T(8,128)(2,1)S(1)}, bf16[96,768]{1,0:T(8,128)(2,1)S(1)}, u32[]{:S(2)}, u32[]{:S(2)}) collective-permute-start(bf16[96,768]{1,0:T(8,128)(2,1)S(1)} %collective-permute-done.4.refs_2_), channel_id=1, source_target_pairs={{0,4},{4,0},{8,12},{12,8},{16,20},{20,16},{24,28},{28,24},{1,5},{5... | collective-permute-start | bytes 442376 | tf_op jit(solution)/shard_map/ppermute | solution.py:368
  22.7 2.4 %collective-permute-start.7 = (bf16[96,768]{1,0:T(8,128)(2,1)S(1)}, bf16[96,768]{1,0:T(8,128)(2,1)S(1)}, u32[]{:S(2)}, u32[]{:S(2)}) collective-permute-start(bf16[96,768]{1,0:T(8,128)(2,1)S(1)} %copy-done.2), channel_id=1, source_target_pairs={{0,4},{4,0},{8,12},{12,8},{16,20},{20,16},{24,28},{28,24},{1,5},{5... | collective-permute-start | bytes 442376 | tf_op jit(solution)/shard_map/ppermute | solution.py:368
  23.8 9.2 %collective-permute-start.13 = (bf16[2,96,768]{2,1,0:T(8,128)(2,1)S(1)}, bf16[2,96,768]{2,1,0:T(8,128)(2,1)S(1)}, u32[]{:S(2)}, u32[]{:S(2)}) collective-permute-start(bf16[2,96,768]{2,1,0:T(8,128)(2,1)S(1)} %get-tuple-element.29), channel_id=1, source_target_pairs={{0,8},{4,12},{8,0},{12,4},{16,24},{20,28},{24,16},{28,20},{1,9},{5... | collective-permute-start | bytes 884744 | tf_op jit(solution)/shard_map/ppermute | solution.py:394
  28.7 10.8 %collective-permute-start.12 = (bf16[4,32,768]{2,1,0:T(8,128)(2,1)S(1)}, bf16[4,32,768]{2,1,0:T(8,128)(2,1)S(1)}, u32[]{:S(2)}, u32[]{:S(2)}) collective-permute-start(bf16[4,32,768]{2,1,0:T(8,128)(2,1)S(1)} %backward.5), channel_id=1, source_target_pairs={{0,3},{1,2},{2,1},{3,0},{4,7},{5,6},{6,5},{7,4},{8,11},{9,10},{10,... | collective-permute-start | bytes 589832 | tf_op jit(solution)/shard_map/ppermute | solution.py:375
  32.5 8.0 %collective-permute-start.11 = (bf16[4,32,768]{2,1,0:T(8,128)(2,1)S(1)}, bf16[4,32,768]{2,1,0:T(8,128)(2,1)S(1)}, u32[]{:S(2)}, u32[]{:S(2)}) collective-permute-start(bf16[4,32,768]{2,1,0:T(8,128)(2,1)S(1)} %backward.4), channel_id=1, source_target_pairs={{0,2},{1,3},{2,0},{3,1},{4,6},{5,7},{6,4},{7,5},{8,10},{9,11},{10,... | collective-permute-start | bytes 589832 | tf_op jit(solution)/shard_map/ppermute | solution.py:375
  33.1 9.2 %collective-permute-start.15 = (bf16[1,96,768]{2,1,0:T(8,128)(2,1)S(1)}, bf16[1,96,768]{2,1,0:T(8,128)(2,1)S(1)}, u32[]{:S(2)}, u32[]{:S(2)}) collective-permute-start(bf16[1,96,768]{2,1,0:T(8,128)(2,1)S(1)} %get-tuple-element.39), channel_id=1, source_target_pairs={{0,16},{4,20},{8,24},{12,28},{16,0},{20,4},{24,8},{28,12},{1,17},{... | collective-permute-start | bytes 442376 | tf_op jit(solution)/shard_map/ppermute | solution.py:394
  36.6 5.9 %collective-permute-start.14 = (bf16[4,32,768]{2,1,0:T(8,128)(2,1)S(1)}, bf16[4,32,768]{2,1,0:T(8,128)(2,1)S(1)}, u32[]{:S(2)}, u32[]{:S(2)}) collective-permute-start(bf16[4,32,768]{2,1,0:T(8,128)(2,1)S(1)} %backward.6), channel_id=1, source_target_pairs={{0,1},{1,0},{2,3},{3,2},{4,5},{5,4},{6,7},{7,6},{8,9},{9,8},{10,11... | collective-permute-start | bytes 589832 | tf_op jit(solution)/shard_map/ppermute | solution.py:375
